TPU v7x, 256 devices: a whole 4x4x8 slice. The times are simulated.
256 devices in a mesh: row: 8 (over x_hi, y), col: 32 (over z, x_lo, core).
Axes of the slice: x: 4 (x_hi: 2, x_lo: 2; x = x_hi * 2 + x_lo), y: 4, z: 8, core: 2. Of those that a mesh axis runs over, the one named last changes fastest.
Arguments:
- layer_inputs: bfloat16 [1024, 4608], P('col', 'row'), may hold values from -6 to 6
- cotangent: bfloat16 [1024, 4608], P('col', 'row'), may hold values from -1.5 to 1.5
- gate_saved: bfloat16 [1024, 36864], P('row', 'col'), may hold values from -6 to 6
- up_saved: bfloat16 [1024, 36864], P('row', 'col'), may hold values from -6 to 6
- gate_weight: bfloat16 [4608, 36864], P('row', 'col'), may hold values from -0.09375 to 0.09375
- up_weight: bfloat16 [4608, 36864], P('row', 'col'), may hold values from -0.09375 to 0.09375
- down_weight: bfloat16 [36864, 4608], P('col', 'row'), may hold values from -0.03125 to 0.03125
Outputs:
- input_grad: bfloat16 [1024, 4608], P('col', 'row')
- gate_weight_grad: bfloat16 [4608, 36864], P('row', 'col')
- up_weight_grad: bfloat16 [4608, 36864], P('row', 'col')
- down_weight_grad: bfloat16 [36864, 4608], P('col', 'row')
All inputs are finite; a program needn't handle non-finite values.
Results may differ from a plain program's by a relative error of at most 0.005.
Values may be sent and summed in bfloat16 or wider, within the bound.
A program may use at most 64 MiB of HBM per device.

v0:
```python
import jax
import jax.numpy as jnp
from jax import lax
from jax.sharding import PartitionSpec as P

SCALE_INNER = 0.7978845608028654
CUBIC_COEF = 0.044715


def gelu_parts(gate_value):
    inner_term = SCALE_INNER * (gate_value + CUBIC_COEF * gate_value * gate_value * gate_value)
    tangent = jnp.tanh(inner_term)
    gelu_value = 0.5 * gate_value * (1.0 + tangent)
    gelu_slope = 0.5 * (1.0 + tangent) + 0.5 * gate_value * (
        1.0 - tangent * tangent
    ) * SCALE_INNER * (1.0 + 3.0 * CUBIC_COEF * gate_value * gate_value)
    return (gelu_value, gelu_slope)


def contract_first(first_operand, second_operand):
    return lax.dot_general(
        first_operand, second_operand, (((0,), (0,)), ((), ())), preferred_element_type=jnp.float32
    )


def contract_last(first_operand, second_operand):
    return lax.dot_general(
        first_operand, second_operand, (((1,), (1,)), ((), ())), preferred_element_type=jnp.float32
    )


def activations(gate_saved, up_saved):
    gate_value = gate_saved.astype(jnp.float32)
    up_value = up_saved.astype(jnp.float32)
    gelu_value, gelu_slope = gelu_parts(gate_value)
    hidden = (gelu_value * up_value).astype(jnp.bfloat16)
    return (hidden, gelu_value, gelu_slope, up_value)


def unit_grads(hidden_grad, gelu_value, gelu_slope, up_value):
    gate_grad = (hidden_grad * up_value * gelu_slope).astype(jnp.bfloat16)
    up_grad = (hidden_grad * gelu_value).astype(jnp.bfloat16)
    return (gate_grad, up_grad)


def body(layer_inputs, cotangent, gate_saved, up_saved, gate_weight, up_weight, down_weight):
    cotangent_all = lax.all_gather(cotangent, "col", axis=0, tiled=True)
    hidden_own, gelu_value, gelu_slope, up_value = activations(gate_saved, up_saved)
    block = cotangent_all
    down_grad = contract_first(lax.all_gather(hidden_own, "row", axis=0, tiled=True), block)
    block = cotangent_all
    hidden_grad = lax.psum_scatter(
        contract_last(block, down_weight), "row", scatter_dimension=0, tiled=True
    )
    gate_grad, up_grad = unit_grads(hidden_grad, gelu_value, gelu_slope, up_value)
    gate_grad_all, up_grad_all = (
        lax.all_gather(gate_grad, "row", axis=0, tiled=True),
        lax.all_gather(up_grad, "row", axis=0, tiled=True),
    )
    inputs_all = lax.all_gather(layer_inputs, "col", axis=0, tiled=True)
    gate_weight_grad = contract_first(inputs_all, gate_grad_all).astype(jnp.bfloat16)
    up_weight_grad = contract_first(inputs_all, up_grad_all).astype(jnp.bfloat16)
    input_grad = lax.psum_scatter(
        contract_last(gate_grad_all, gate_weight) + contract_last(up_grad_all, up_weight),
        "col",
        scatter_dimension=0,
        tiled=True,
    ).astype(jnp.bfloat16)
    return (input_grad, gate_weight_grad, up_weight_grad, down_grad.astype(jnp.bfloat16))


def solution(mesh):
    placed = (
        P("col", "row"),
        P("col", "row"),
        P("row", "col"),
        P("row", "col"),
        P("row", "col"),
        P("row", "col"),
        P("col", "row"),
    )
    return jax.shard_map(
        body,
        mesh=mesh,
        in_specs=placed,
        out_specs=(P("col", "row"), P("row", "col"), P("row", "col"), P("col", "row")),
        check_vma=False,
    )
```

profile of v0, /device:TPU:1, one launch (start us, length us, event | category | flops | bytes accessed | tf_op | source)
XLA Modules:
  0.0 553.3 jit_solution(10736864012016205563)
XLA Ops:
  7.2 0.0 copy-start
  7.2 0.0 all-gather.6.cloned.1.call-start
  7.2 0.7 all-gather.6.cloned.1.call-update
  7.9 0.0 reduce-scatter.3.cloned.1.call-start
  8.0 70.2 %all-gather.6.cloned.1.call-done = bf16[1024,576]{1,0:T(8,128)(2,1)} async-done(((bf16[32,576]{1,0:T(8,128)(2,1)}), bf16[1024,576]{1,0:T(8,128)(2,1)}) %all-gather.6.cloned.1.call-update) | async-done | bytes 1179664 | tf_op jit(solution)/shard_map/all_gather | solution.py:47
  78.2 0.0 copy-done
  78.2 5.6 %fusion.13 = f32[1024,1152]{1,0:T(8,128)} fusion(bf16[1024,576]{1,0:T(8,128)(2,1)} %all-gather.6.cloned.1.call-done, bf16[1152,576]{0,1:T(8,128)(2,1)S(1)} %copy-done), kind=kOutput, calls=%fused_computation.27 | convolution fusion | flops 1358954496 | bytes 7225344 | tf_op jit(solution)/shard_map/dot_general | solution.py:27
  83.8 0.0 copy-start.1
  83.8 0.0 copy-start.2
  83.8 0.0 reduce-scatter.3.cloned.1.call-update
  83.8 0.0 copy-start.4
  83.8 0.0 all-gather.8.cloned.1.call-start
  83.9 91.3 %reduce-scatter.3.cloned.1.call-done = f32[128,1152]{1,0:T(8,128)} async-done(((f32[1024,1152]{1,0:T(8,128)}), f32[128,1152]{1,0:T(8,128)}) %reduce-scatter.3.cloned.1.call-update) | async-done | bytes 589840 | tf_op jit(solution)/shard_map/reduce_scatter | solution.py:52
  175.2 0.0 copy-done.1
  175.2 0.0 copy-done.2
  175.2 2.6 multiply_convert_fusion
  177.7 0.0 all-gather.8.cloned.1.call-update
  177.8 0.0 all-gather.10.cloned.1.call-start
  177.8 0.5 all-gather.10.cloned.1.call-update
  178.3 0.0 all-gather.12.cloned.1.call-start
  178.4 0.5 all-gather.12.cloned.1.call-update
  178.9 0.0 all-gather.14.cloned.1.call-start
  179.0 0.5 all-gather.14.cloned.1.call-update
  179.5 0.0 reduce-scatter.5.cloned.1.call-start
  179.6 59.3 %all-gather.8.cloned.1.call-done = bf16[1024,1152]{1,0:T(8,128)(2,1)} async-done(((bf16[128,1152]{1,0:T(8,128)(2,1)}), bf16[1024,1152]{1,0:T(8,128)(2,1)}) %all-gather.8.cloned.1.call-update) | async-done | bytes 2359312 | tf_op jit(solution)/shard_map/all_gather | solution.py:57
  238.8 0.0 copy-done.4
  238.8 5.3 fusion.14
  244.2 56.7 %all-gather.10.cloned.1.call-done = bf16[1024,1152]{1,0:T(8,128)(2,1)} async-done(((bf16[128,1152]{1,0:T(8,128)(2,1)}), bf16[1024,1152]{1,0:T(8,128)(2,1)}) %all-gather.10.cloned.1.call-update) | async-done | bytes 2359312 | tf_op jit(solution)/shard_map/all_gather | solution.py:58
  300.9 6.5 %convolution_add_fusion = f32[1024,576]{1,0:T(8,128)} fusion(f32[1024,576]{1,0:T(8,128)} %fusion.14, bf16[1024,1152]{1,0:T(8,128)(2,1)} %all-gather.10.cloned.1.call-done, bf16[576,1152]{1,0:T(8,128)(2,1)} %param.12), kind=kOutput, calls=%fused_computation.5 | convolution fusion | flops 1359544320 | bytes 8404992 | tf_op jit(solution)/shard_map/dot_general | solution.py:27
  307.4 0.0 reduce-scatter.5.cloned.1.call-update
  307.4 58.0 %all-gather.12.cloned.1.call-done = bf16[1024,576]{1,0:T(8,128)(2,1)} async-done(((bf16[32,576]{1,0:T(8,128)(2,1)}), bf16[1024,576]{1,0:T(8,128)(2,1)}) %all-gather.12.cloned.1.call-update) | async-done | bytes 1179664 | tf_op jit(solution)/shard_map/all_gather | solution.py:60
  365.5 0.0 copy-start.3
  365.5 0.0 copy-start.6
  365.5 5.0 fusion
  370.4 0.0 copy-done.3
  370.4 0.0 copy-done.6
  370.5 0.0 copy-start.5
  370.5 2.9 fusion.1
  373.3 54.5 %all-gather.14.cloned.1.call-done = bf16[1024,1152]{1,0:T(8,128)(2,1)} async-done(((bf16[128,1152]{1,0:T(8,128)(2,1)}), bf16[1024,1152]{1,0:T(8,128)(2,1)}) %all-gather.14.cloned.1.call-update) | async-done | bytes 2359312 | tf_op jit(solution)/shard_map/all_gather | solution.py:50
  427.9 0.0 copy-done.5
  427.9 4.5 convolution_convert_fusion
  432.3 112.7 %reduce-scatter.5.cloned.1.call-done = f32[32,576]{1,0:T(8,128)} async-done(((f32[1024,576]{1,0:T(8,128)}), f32[32,576]{1,0:T(8,128)}) %reduce-scatter.5.cloned.1.call-update) | async-done | bytes 73744 | tf_op jit(solution)/shard_map/reduce_scatter | solution.py:63
  545.0 1.5 convert_element_type.37
Async XLA Ops:
  7.2 71.0 %copy-start = (bf16[1152,576]{0,1:T(8,128)(2,1)S(1)}, bf16[1152,576]{0,1:T(8,128)(2,1)}, u32[]{:S(2)}) copy-start(bf16[1152,576]{0,1:T(8,128)(2,1)} %param.13) | copy-start | bytes 3981316
  7.2 71.0 %all-gather.6.cloned.1.call-start = ((), (), s32[]{:S(2)}) async-start(), calls=%async_computation.2 | async-start | bytes 1351680 | tf_op jit(solution)/shard_map/all_gather | solution.py:47
  7.9 167.3 %reduce-scatter.3.cloned.1.call-start = ((), (), s32[]{:S(2)}) async-start(), calls=%async_computation.3 | async-start | bytes 5308416 | tf_op jit(solution)/shard_map/reduce_scatter | solution.py:52
  83.8 91.4 %copy-start.1 = (bf16[128,1152]{1,0:T(8,128)(2,1)S(1)}, bf16[128,1152]{1,0:T(8,128)(2,1)}, u32[]{:S(2)}) copy-start(bf16[128,1152]{1,0:T(8,128)(2,1)} %param.9) | copy-start | bytes 884740
  83.8 91.4 %copy-start.2 = (bf16[128,1152]{1,0:T(8,128)(2,1)S(1)}, bf16[128,1152]{1,0:T(8,128)(2,1)}, u32[]{:S(2)}) copy-start(bf16[128,1152]{1,0:T(8,128)(2,1)} %param.10) | copy-start | bytes 884740
  83.8 155.0 %copy-start.4 = (bf16[576,1152]{1,0:T(8,128)(2,1)S(1)}, bf16[576,1152]{1,0:T(8,128)(2,1)}, u32[]{:S(2)}) copy-start(bf16[576,1152]{1,0:T(8,128)(2,1)} %param.11) | copy-start | bytes 3981316
  83.8 155.0 %all-gather.8.cloned.1.call-start = ((), (), s32[]{:S(2)}) async-start(), calls=%async_computation.4 | async-start | bytes 2654208 | tf_op jit(solution)/shard_map/all_gather | solution.py:57
  177.8 123.1 %all-gather.10.cloned.1.call-start = ((), (), s32[]{:S(2)}) async-start(), calls=%async_computation.5 | async-start | bytes 2654208 | tf_op jit(solution)/shard_map/all_gather | solution.py:58
  178.3 187.1 %all-gather.12.cloned.1.call-start = ((), (), s32[]{:S(2)}) async-start(), calls=%async_computation.7 | async-start | bytes 1351680 | tf_op jit(solution)/shard_map/all_gather | solution.py:60
  178.9 248.9 %all-gather.14.cloned.1.call-start = ((), (), s32[]{:S(2)}) async-start(), calls=%async_computation.8 | async-start | bytes 2654208 | tf_op jit(solution)/shard_map/all_gather | solution.py:50
  179.5 365.5 %reduce-scatter.5.cloned.1.call-start = ((), (), s32[]{:S(2)}) async-start(), calls=%async_computation.6 | async-start | bytes 2703360 | tf_op jit(solution)/shard_map/reduce_scatter | solution.py:63
  365.5 5.0 copy-start.3
  365.5 5.0 copy-start.6
  370.5 57.4 %copy-start.5 = (bf16[1024,576]{1,0:T(8,128)(2,1)S(1)}, bf16[1024,576]{1,0:T(8,128)(2,1)}, u32[]{:S(2)}) copy-start(bf16[1024,576]{1,0:T(8,128)(2,1)} %all-gather.6.cloned.1.call-done) | copy-start | bytes 3538948
Sparse Core Ops, SparseCore 0:
  9.9 68.2 all-gather.5
  83.9 91.1 reduce-scatter.2
  178.4 60.4 all-gather.7
  241.8 58.9 all-gather.9
  302.6 62.8 all-gather.11
  367.9 59.9 all-gather.13
  430.4 114.5 reduce-scatter.4
where the time goes:
time: 556 us; the launch traced here: 553 us
  waiting for transfers between devices  505 us (91%)
  matrix products  29.7 us (5%)
  between operations  14.2 us (3%)
    reduce_scatter x1, waiting for transfers between devices, body(): lax.psum_scatter(contract_last(gate_grad_all, gate_weight) + contract_las...  113 us
    reduce_scatter x1, waiting for transfers between devices, body(): lax.psum_scatter(contract_last(block, down_weight), 'row', scatter_dimens...  91.3 us
    all_gather x1, waiting for transfers between devices, body(): cotangent_all = lax.all_gather(cotangent, 'col', axis=0, tiled=True)  70.2 us
    all_gather x1, waiting for transfers between devices, body(): lax.all_gather(gate_grad, 'row', axis=0, tiled=True)  59.3 us
    all_gather x1, waiting for transfers between devices, body(): inputs_all = lax.all_gather(layer_inputs, 'col', axis=0, tiled=True)  58 us
    all_gather x1, waiting for transfers between devices, body(): lax.all_gather(up_grad, 'row', axis=0, tiled=True)  56.7 us
    all_gather x1, waiting for transfers between devices, body(): lax.all_gather(hidden_own, 'row', axis=0, tiled=True)  54.5 us
    dot_general x3, matrix products, contract_last(): lax.dot_general(first_operand, second_operand, (((1,), (1,)), ((), ())),...  17.4 us
  transfers between devices with their start and end apart: 7, of which 7 were waited for; matrix products, arithmetic and copies ran while one was open for 4% of the time, Pallas kernels for 0%

commit v1 on v0

v1 whole, which is shorter than its diff:
```python
import functools

import jax
import jax.numpy as jnp
from jax import lax
from jax.experimental import pallas as pl
from jax.experimental.pallas import tpu as pltpu
from jax.sharding import PartitionSpec as P

SCALE_INNER = 0.7978845608028654
CUBIC_COEF = 0.044715
MESH = pl.DeviceIdType.MESH
BF16 = jnp.bfloat16
F32 = jnp.float32

W = 576
U = 1152
NT = 384
N_REMOTE = 112


def gelu_parts(gate_value):
    inner_term = SCALE_INNER * (gate_value + CUBIC_COEF * gate_value * gate_value * gate_value)
    tangent = jnp.tanh(inner_term)
    gelu_value = 0.5 * gate_value * (1.0 + tangent)
    gelu_slope = 0.5 * (1.0 + tangent) + 0.5 * gate_value * (
        1.0 - tangent * tangent
    ) * SCALE_INNER * (1.0 + 3.0 * CUBIC_COEF * gate_value * gate_value)
    return (gelu_value, gelu_slope)


def dot_nt(a, b):
    return lax.dot_general(a, b, (((1,), (1,)), ((), ())), preferred_element_type=F32)


def dot_tn(a, b):
    return lax.dot_general(a, b, (((0,), (0,)), ((), ())), preferred_element_type=F32)


def kernel(
    inp_h, cot_h, g_h, u_h, gw_h, uw_h, dw_h,
    ig_o, gwg_o, uwg_o, dwg_o,
    cot_all, inp_all, h_all, gg_all, ug_all, part,
    g_v, u_v, dw_v, gw_v, uw_v, val, slope_up,
    ry_relay, ry_full, sy, sx, rx, q_own,
    ig_part, ig_core, ig_send, ig_recv, ig_red, ig_fin, ig_out,
    gwg_v, uwg_v, dwg_v,
    lsem, ssem, rsem,
):
    row, col = lax.axis_index("row"), lax.axis_index("col")
    xh, y = lax.div(row, 4), lax.rem(row, 4)
    z, xl, co = lax.div(col, 4), lax.rem(lax.div(col, 2), 2), lax.rem(col, 2)
    y_next, y_prev, y_far = lax.rem(y + 1, 4), lax.rem(y + 3, 4), lax.rem(y + 2, 4)
    zs = [lax.rem(z + k, 8) for k in range(8)]

    yp = (xh * 4 + y_next, col)
    ym = (xh * 4 + y_prev, col)
    x2 = ((1 - xh) * 4 + y, col)
    mate = (row, col + 1 - 2 * co)
    side = (row, z * 4 + (1 - xl) * 2 + co)
    zd = [None] + [(row, zs[k] * 4 + xl * 2 + co) for k in range(1, 8)]
    partners = [yp, ym, x2, mate, side] + zd[1:]

    def load(i, src, dst):
        cp = pltpu.make_async_copy(src, dst, lsem.at[i])
        cp.start()
        return cp

    l_cot = load(0, cot_h, cot_all.at[z, xl, co])
    l_g = load(1, g_h, g_v)
    l_u = load(2, u_h, u_v)
    l_inp = load(3, inp_h, inp_all.at[z, xl, co])
    l_dw = load(4, dw_h, dw_v)
    l_gw = load(5, gw_h, gw_v)
    l_uw = load(6, uw_h, uw_v)

    barrier = pltpu.get_barrier_semaphore()
    for d in partners:
        pl.semaphore_signal(barrier, inc=1, device_id=d, device_id_type=MESH)
    pl.semaphore_wait(barrier, len(partners))

    sends = []

    def send(src, dst, device):
        i = len(sends)
        cp = pltpu.make_async_remote_copy(
            src_ref=src, dst_ref=dst, send_sem=ssem.at[i], recv_sem=rsem.at[i],
            device_id=device, device_id_type=MESH,
        )
        cp.start()
        sends.append(cp)
        return cp

    def col_start(buf):
        return send(buf.at[z, xl, co], buf.at[z, xl, co], side)

    def col_pair(buf, k, device):
        return send(buf.at[zs[k], :, co], buf.at[zs[k], :, co], device)

    def col_steps(buf, first):
        first.wait_recv()
        up = col_pair(buf, 0, zd[1])
        down = col_pair(buf, 0, zd[7])
        cores = [col_pair(buf, 0, mate)]
        yield
        for s in (1, 2, 3):
            up.wait_recv()
            if s < 3:
                up = col_pair(buf, 8 - s, zd[1])
            else:
                up = send(buf.at[zs[5], 0, co], buf.at[zs[5], 0, co], zd[1])
            cores.append(col_pair(buf, 8 - s, mate))
            down.wait_recv()
            if s < 3:
                down = col_pair(buf, s, zd[7])
            else:
                down = send(buf.at[zs[3], 1, co], buf.at[zs[3], 1, co], zd[7])
            cores.append(col_pair(buf, s, mate))
            yield
        up.wait_recv()
        down.wait_recv()
        cores.append(col_pair(buf, 4, mate))
        yield
        for cp in cores:
            cp.wait_recv()
        yield

    l_cot.wait()
    cot_first = col_start(cot_all)

    l_g.wait()
    l_u.wait()

    def act(i, carry):
        rows = pl.ds(pl.multiple_of(i * 32, 32), 32)
        gate_value = g_v[rows].astype(F32)
        up_value = u_v[rows].astype(F32)
        gelu_value, gelu_slope = gelu_parts(gate_value)
        h_all[xh, y, rows] = (gelu_value * up_value).astype(BF16)
        val[rows] = gelu_value
        slope_up[rows] = up_value * gelu_slope
        return carry

    lax.fori_loop(0, 4, act, 0)

    h_up = send(h_all.at[xh, y], h_all.at[xh, y], yp)
    h_down = send(h_all.at[xh, y], h_all.at[xh, y], ym)
    h_x = [send(h_all.at[xh, y], h_all.at[xh, y], x2)]
    l_inp.wait()
    inp_first = col_start(inp_all)

    steps = col_steps(cot_all, cot_first)
    for _ in range(5):
        next(steps)

    A, B = pl.ds(0, 64), pl.ds(64, 64)
    h_up.wait_recv()
    h_ru = send(h_all.at[xh, y_prev, A], h_all.at[xh, y_prev, A], yp)
    h_x.append(send(h_all.at[xh, y_prev], h_all.at[xh, y_prev], x2))
    h_down.wait_recv()
    h_rd = send(h_all.at[xh, y_next, B], h_all.at[xh, y_next, B], ym)
    h_x.append(send(h_all.at[xh, y_next], h_all.at[xh, y_next], x2))

    next(steps)
    inp_steps = col_steps(inp_all, inp_first)

    l_dw.wait()

    def partial(h):
        def tile(n, carry):
            cols = pl.ds(pl.multiple_of(n * NT, 128), NT)
            lhs = cot_all[:, h].reshape(512, W)
            part[h, :, :, :, cols] = dot_nt(lhs, dw_v[cols]).astype(BF16).reshape(2, 4, 64, NT)
            return carry

        lax.fori_loop(0, U // NT, tile, 0)

    lo, hi = pl.ds(0, 32), pl.ds(32, 32)

    def rs_first(h):
        relay_up = send(part.at[h, :, y_far, lo], ry_relay.at[h, 0], yp)
        relay_down = send(part.at[h, :, y_far, hi], ry_relay.at[h, 1], ym)
        direct_up = send(part.at[h, :, y_next, hi], ry_full.at[h, 0, :, hi], yp)
        direct_down = send(part.at[h, :, y_prev, lo], ry_full.at[h, 1, :, lo], ym)
        return relay_up, relay_down, direct_up, direct_down

    def rs_second(h, relay_up, relay_down):
        relay_up.wait_recv()
        sy[h, 0] = (part[h, :, y_next, 0:32].astype(F32) + ry_relay[h, 0].astype(F32)).astype(BF16)
        both_up = send(sy.at[h, 0], ry_full.at[h, 0, :, lo], yp)
        relay_down.wait_recv()
        sy[h, 1] = (part[h, :, y_prev, 32:64].astype(F32) + ry_relay[h, 1].astype(F32)).astype(BF16)
        both_down = send(sy.at[h, 1], ry_full.at[h, 1, :, hi], ym)
        return both_up, both_down

    def rs_third(h, waits):
        for cp in waits:
            cp.wait_recv()

        def total(which):
            return (
                part[h, which, y].astype(F32)
                + ry_full[h, 0, which].astype(F32)
                + ry_full[h, 1, which].astype(F32)
            )

        sx[h] = total(1 - xh).astype(BF16)
        cp = send(sx.at[h], rx.at[h], x2)
        q_own[h] = total(xh)
        return cp

    def grads(h, cp):
        cp.wait_recv()
        hidden_grad = q_own[h] + rx[h].astype(F32)
        gg_all[h, xh, y] = (hidden_grad * slope_up[h * 64 : h * 64 + 64]).astype(BF16)
        ug_all[h, xh, y] = (hidden_grad * val[h * 64 : h * 64 + 64]).astype(BF16)

    def ag(ref, h, k, yy, device, rows=None):
        r = ref.at[h, k, yy] if rows is None else ref.at[h, k, yy, rows]
        return send(r, r, device)

    class Gather:
        def start(self, h):
            self.h = h
            self.gx = ag(gg_all, h, xh, y, x2)
            self.gu = [ag(gg_all, h, xh, y, yp)]
            self.gd = [ag(gg_all, h, xh, y, ym)]
            self.uu = ag(ug_all, h, xh, y, yp)
            self.ud = ag(ug_all, h, xh, y, ym)
            self.ux = [ag(ug_all, h, xh, y, x2)]

        def across(self):
            h = self.h
            self.gx.wait_recv()
            self.gu.append(ag(gg_all, h, 1 - xh, y, yp))
            self.gd.append(ag(gg_all, h, 1 - xh, y, ym))

        def relay(self):
            h = self.h
            self.rest = []
            self.gu[0].wait_recv()
            self.rest.append(ag(gg_all, h, xh, y_prev, yp, lo))
            self.gd[0].wait_recv()
            self.rest.append(ag(gg_all, h, xh, y_next, ym, hi))
            self.uu.wait_recv()
            self.ru = ag(ug_all, h, xh, y_prev, yp, lo)
            self.ux.append(ag(ug_all, h, xh, y_prev, x2))
            self.ud.wait_recv()
            self.rd = ag(ug_all, h, xh, y_next, ym, hi)
            self.ux.append(ag(ug_all, h, xh, y_next, x2))
            self.gu[1].wait_recv()
            self.rest.append(ag(gg_all, h, 1 - xh, y_prev, yp, lo))
            self.gd[1].wait_recv()
            self.rest.append(ag(gg_all, h, 1 - xh, y_next, ym, hi))

        def last(self):
            self.ru.wait_recv()
            self.rd.wait_recv()
            self.ux.append(ag(ug_all, self.h, xh, y_far, x2))

        def done(self):
            for cp in self.rest + self.ux:
                cp.wait_recv()

    def input_grad(h):
        total = dot_nt(gg_all[h].reshape(512, U), gw_v[...])
        total += dot_nt(ug_all[h].reshape(512, U), uw_v[...])
        ig_part[h] = total.reshape(8, 2, 32, W)
        return send(ig_part.at[h, :, 1 - co], ig_core.at[h], mate)

    def input_grad_send(h, cp):
        cp.wait_recv()
        ig_send[h] = (ig_part[h, :, co] + ig_core[h]).astype(BF16)
        return [send(ig_send.at[h, zs[k]], ig_recv.at[h, k - 1], zd[k]) for k in range(1, 8)]

    def input_grad_sum(h, cps):
        total = ig_part[h, z, co] + ig_core[h, z]
        for cp in cps:
            cp.wait_recv()
        for k in range(7):
            total += ig_recv[h, k].astype(F32)
        ig_red[h] = total

    def weight_grad(grad_all, out):
        def tile(n, carry):
            cols = pl.ds(pl.multiple_of(n * NT, 128), NT)
            total = dot_tn(inp_all[:, 0].reshape(512, W), grad_all[0, :, :, :, cols].reshape(512, NT))
            total += dot_tn(inp_all[:, 1].reshape(512, W), grad_all[1, :, :, :, cols].reshape(512, NT))
            out[:, cols] = total.astype(BF16)
            return carry

        lax.fori_loop(0, U // NT, tile, 0)

    def down_grad():
        def tile(n, carry):
            cols = pl.ds(pl.multiple_of(n * NT, 128), NT)
            lhs = h_all[:, :, :, cols].reshape(1024, NT)
            dwg_v[cols] = dot_tn(lhs, cot_all[...].reshape(1024, W)).astype(BF16)
            return carry

        lax.fori_loop(0, U // NT, tile, 0)

    partial(0)
    ru0, rd0, du0, dd0 = rs_first(0)
    next(inp_steps)
    partial(1)
    next(inp_steps)
    bu0, bd0 = rs_second(0, ru0, rd0)
    ru1, rd1, du1, dd1 = rs_first(1)
    h_ru.wait_recv()
    h_rd.wait_recv()
    h_x.append(send(h_all.at[xh, y_far], h_all.at[xh, y_far], x2))
    next(inp_steps)
    x0 = rs_third(0, (du0, dd0, bu0, bd0))
    bu1, bd1 = rs_second(1, ru1, rd1)
    for _ in range(3):
        next(inp_steps)
    grads(0, x0)
    g0, g1 = Gather(), Gather()
    g0.start(0)
    x1 = rs_third(1, (du1, dd1, bu1, bd1))
    g0.across()
    grads(1, x1)
    for cp in h_x:
        cp.wait_recv()
    down_grad()
    outs = [load(7, dwg_v, dwg_o)]
    g0.relay()
    g1.start(1)
    g0.last()
    g1.across()
    l_gw.wait()
    l_uw.wait()
    g0.done()
    c0 = input_grad(0)
    g1.relay()
    z0 = input_grad_send(0, c0)
    g1.last()
    input_grad_sum(0, z0)
    g1.done()
    c1 = input_grad(1)
    z1 = input_grad_send(1, c1)
    weight_grad(gg_all, gwg_v)
    outs.append(load(8, gwg_v, gwg_o))
    weight_grad(ug_all, uwg_v)
    outs.append(load(9, uwg_v, uwg_o))
    input_grad_sum(1, z1)
    fin = send(ig_red.at[1 - xl], ig_fin, side)
    fin.wait_recv()
    ig_out[...] = (ig_red[xl] + ig_fin[...]).astype(BF16)
    outs.append(load(10, ig_out, ig_o))
    for cp in sends:
        cp.wait_send()
    for cp in outs:
        cp.wait()


def body(layer_inputs, cotangent, gate_saved, up_saved, gate_weight, up_weight, down_weight):
    any_spec = pl.BlockSpec(memory_space=pl.ANY)

    def bf(*shape):
        return pltpu.VMEM(shape, BF16)

    def f32(*shape):
        return pltpu.VMEM(shape, F32)

    return pl.pallas_call(
        kernel,
        out_shape=(
            jax.ShapeDtypeStruct((32, W), BF16),
            jax.ShapeDtypeStruct((W, U), BF16),
            jax.ShapeDtypeStruct((W, U), BF16),
            jax.ShapeDtypeStruct((U, W), BF16),
        ),
        in_specs=[any_spec] * 7,
        out_specs=[any_spec] * 4,
        scratch_shapes=[
            bf(8, 2, 2, 32, W), bf(8, 2, 2, 32, W), bf(2, 4, 128, U),
            bf(2, 2, 4, 64, U), bf(2, 2, 4, 64, U), bf(2, 2, 4, 64, U),
            bf(128, U), bf(128, U), bf(U, W), bf(W, U), bf(W, U), f32(128, U), f32(128, U),
            bf(2, 2, 2, 32, U), bf(2, 2, 2, 64, U), bf(2, 2, 2, 32, U), bf(2, 64, U), bf(2, 64, U), f32(2, 64, U),
            f32(2, 8, 2, 32, W), f32(2, 8, 32, W), bf(2, 8, 32, W), bf(2, 7, 32, W), f32(2, 32, W), f32(32, W), bf(32, W),
            bf(W, U), bf(W, U), bf(U, W),
            pltpu.SemaphoreType.DMA((11,)),
            pltpu.SemaphoreType.DMA((N_REMOTE,)),
            pltpu.SemaphoreType.DMA((N_REMOTE,)),
        ],
        compiler_params=pltpu.CompilerParams(
            collective_id=0, has_side_effects=True, vmem_limit_bytes=56 * 2**20
        ),
        cost_estimate=pl.CostEstimate(flops=8 * 10**9, bytes_accessed=9 * 10**6, transcendentals=150000),
    )(layer_inputs, cotangent, gate_saved, up_saved, gate_weight, up_weight, down_weight)


def solution(mesh):
    placed = (
        P("col", "row"),
        P("col", "row"),
        P("row", "col"),
        P("row", "col"),
        P("row", "col"),
        P("row", "col"),
        P("col", "row"),
    )
    return jax.shard_map(
        body,
        mesh=mesh,
        in_specs=placed,
        out_specs=(P("col", "row"), P("row", "col"), P("row", "col"), P("col", "row")),
        check_vma=False,
    )
```

time: 556 us -> 126 us (0.23)
  waiting for transfers between devices: 505 us -> 0 us
  Pallas kernels: 0 us -> 115 us
  matrix products: 29.7 us -> 0 us
  between operations: 14.2 us -> 0.66 us
  local copies, waits for them, and re-layouts: 0.03 us -> 8.77 us
    all_gather x5 -> x0, waiting for transfers between devices: 299 us -> none  [the longest x1 70.2 us: body(): cotangent_all = lax.all_gather(cotangent, 'col', axis=0, tiled=True)]
    reduce_scatter x2 -> x0, waiting for transfers between devices: 204 us -> none  [the longest x1 113 us: body(): lax.psum_scatter(contract_last(gate_grad_all, gate_weight) + contract_las...]
    pallas_call x0 -> x1, Pallas kernels: none -> 115 us  [body(): pl.pallas_call(kernel, out_shape=(jax.ShapeDtypeStruct((32, W), BF16), ja...]
    dot_general x6 -> x0, matrix products: 29.7 us -> none  [the longest x3 17.4 us: contract_last(): lax.dot_general(first_operand, second_operand, (((1,), (1,)), ((), ())),...]
    unnamed x14 -> x10, local copies, waits for them, and re-layouts: 0.03 us -> 6.1 us
  transfers between devices with their start and end apart: 7 -> 0, of which waited for: 7 -> 0; matrix products, arithmetic and copies ran while one was open for 4% -> 0% of each run, Pallas kernels for 0% -> 0%
where the time goes in v1:
time: 126 us; the launch traced here: 125 us
  Pallas kernels  115 us (91%)
  local copies, waits for them, and re-layouts  8.77 us (7%)
    pallas_call x1, Pallas kernels, body(): pl.pallas_call(kernel, out_shape=(jax.ShapeDtypeStruct((32, W), BF16), ja...  115 us
    unnamed x10, local copies, waits for them, and re-layouts  6.1 us
    pallas_call x1, local copies, waits for them, and re-layouts, body(): pl.pallas_call(kernel, out_shape=(jax.ShapeDtypeStruct((32, W), BF16), ja...  2.67 us

profile of v1, /device:TPU:1, one launch (start us, length us, event | category | flops | bytes accessed | tf_op | source)
XLA Modules:
  0.0 124.9 jit_solution(10348091377681698870)
XLA Ops:
  0.6 2.6 %copy.11.dw_h = bf16[1152,576]{1,0:T(8,128)(2,1)} copy(bf16[1152,576]{0,1:T(8,128)(2,1)} %param.13) | data formatting | bytes 2654208 | tf_op args[6]
  3.2 115.5 %shard_map.102 = (bf16[32,576]{1,0:T(8,128)(2,1)}, bf16[576,1152]{1,0:T(8,128)(2,1)}, bf16[576,1152]{1,0:T(8,128)(2,1)}, bf16[1152,576]{1,0:T(8,128)(2,1)}) custom-call(bf16[32,576]{1,0:T(8,128)(2,1)} %inp_h.1, bf16[32,576]{1,0:T(8,128)(2,1)} %cot_h.1, bf16[128,1152]{1,0:T(8,128)(2,1)} %g_h.1, bf16[128,1152]{1,0:T(8,128)(2,1)} %u_h.1, ...), custom_call_target="tpu_custom_call" | custom-call | flops 8000000000 | bytes 9000000 | tf_op jit(solution)/shard_map/pallas_call | solution.py:367
  118.7 0.0 copy-start.2
  118.8 0.0 copy-start.1
  118.8 2.7 %copy.12 = bf16[1152,576]{0,1:T(8,128)(2,1)} copy(bf16[1152,576]{1,0:T(8,128)(2,1)} %get-tuple-element.7) | data formatting | bytes 2654208 | tf_op jit(solution)/shard_map/pallas_call | solution.py:367
  121.4 0.0 copy-done.2
  121.4 0.6 copy.16
  122.1 0.0 copy-done.1
  122.1 0.0 copy-start
  122.1 1.1 copy.17
  123.1 0.7 copy-done
  123.9 1.1 copy.18
Async XLA Ops:
  118.7 2.7 %copy-start.2 = (bf16[32,576]{1,0:T(8,128)(2,1)S(1)}, bf16[32,576]{1,0:T(8,128)(2,1)}, u32[]{:S(2)}) copy-start(bf16[32,576]{1,0:T(8,128)(2,1)} %get-tuple-element.12) | copy-start | bytes 110596
  118.8 3.3 %copy-start.1 = (bf16[576,1152]{1,0:T(8,128)(2,1)S(1)}, bf16[576,1152]{1,0:T(8,128)(2,1)}, u32[]{:S(2)}) copy-start(bf16[576,1152]{1,0:T(8,128)(2,1)} %get-tuple-element.13) | copy-start | bytes 3981316
  122.1 1.8 %copy-start = (bf16[576,1152]{1,0:T(8,128)(2,1)S(1)}, bf16[576,1152]{1,0:T(8,128)(2,1)}, u32[]{:S(2)}) copy-start(bf16[576,1152]{1,0:T(8,128)(2,1)} %get-tuple-element.14) | copy-start | bytes 3981316

commit v2 on v0

v2 whole, which is shorter than its diff:
```python
import functools

import jax
import jax.numpy as jnp
from jax import lax
from jax.experimental import pallas as pl
from jax.experimental.pallas import tpu as pltpu
from jax.sharding import PartitionSpec as P

SCALE_INNER = 0.7978845608028654
CUBIC_COEF = 0.044715
MESH = pl.DeviceIdType.MESH
BF16 = jnp.bfloat16
F32 = jnp.float32

W = 576
U = 1152
NT = 384
N_REMOTE = 140


def gelu_parts(gate_value):
    inner_term = SCALE_INNER * (gate_value + CUBIC_COEF * gate_value * gate_value * gate_value)
    tangent = jnp.tanh(inner_term)
    gelu_value = 0.5 * gate_value * (1.0 + tangent)
    gelu_slope = 0.5 * (1.0 + tangent) + 0.5 * gate_value * (
        1.0 - tangent * tangent
    ) * SCALE_INNER * (1.0 + 3.0 * CUBIC_COEF * gate_value * gate_value)
    return (gelu_value, gelu_slope)


def dot_nt(a, b):
    return lax.dot_general(a, b, (((1,), (1,)), ((), ())), preferred_element_type=F32)


def dot_nn(a, b):
    return lax.dot_general(a, b, (((1,), (0,)), ((), ())), preferred_element_type=F32)


def dot_tn(a, b):
    return lax.dot_general(a, b, (((0,), (0,)), ((), ())), preferred_element_type=F32)


def kernel(
    inp_h, cot_h, g_h, u_h, gw_h, uw_h, dw_h,
    ig_o, gwg_o, uwg_o, dwg_o,
    cot_all, inp_all, g_all, u_all, h_all, hg_all, gg_all, ug_all, val, slope_up, part,
    dw_v, gw_v, uw_v,
    ry_relay, ry_full, sy, sx, rx, q_own,
    ig_part, ig_core, ig_send, ig_recv, ig_red, ig_fin,
    lsem, ssem, rsem,
):
    row, col = lax.axis_index("row"), lax.axis_index("col")
    xh, y = lax.div(row, 4), lax.rem(row, 4)
    z, xl, co = lax.div(col, 4), lax.rem(lax.div(col, 2), 2), lax.rem(col, 2)
    y_next, y_prev, y_far = lax.rem(y + 1, 4), lax.rem(y + 3, 4), lax.rem(y + 2, 4)
    zs = [lax.rem(z + k, 8) for k in range(8)]
    hs = [1 - xl, xl]
    qs = [(1 - xl, 1 - co), (1 - xl, co), (xl, 1 - co), (xl, co)]

    yp = (xh * 4 + y_next, col)
    ym = (xh * 4 + y_prev, col)
    x2 = ((1 - xh) * 4 + y, col)
    mate = (row, col + 1 - 2 * co)
    side = (row, z * 4 + (1 - xl) * 2 + co)
    zd = [None] + [(row, zs[k] * 4 + xl * 2 + co) for k in range(1, 8)]
    near = (1, 7, 2, 6, 3, 5, 4)
    partners = [yp, ym, x2, mate, side] + zd[1:]

    def load(i, src, dst):
        cp = pltpu.make_async_copy(src, dst, lsem.at[i])
        cp.start()
        return cp

    sends = []

    def send(src, dst, device):
        i = len(sends)
        cp = pltpu.make_async_remote_copy(
            src_ref=src, dst_ref=dst, send_sem=ssem.at[i], recv_sem=rsem.at[i],
            device_id=device, device_id_type=MESH,
        )
        cp.start()
        sends.append(cp)
        return cp

    def to(ref, device):
        return send(ref, ref, device)

    def whole(ref):
        return lambda k, yy, half=None: ref.at[k, yy] if half is None else ref.at[k, yy, half]

    def chunk(ref, c):
        h, q = qs[c]

        def piece(k, yy, half=None):
            return ref.at[k, yy, h, q] if half is None else ref.at[k, yy, h, q, pl.ds(16 * half, 16)]

        return piece

    class AcrossFirst:
        def __init__(self, piece):
            self.piece = piece

        def start(self):
            own = self.piece(xh, y)
            self.across_cp = to(own, x2)
            self.up, self.down, self.rest = [to(own, yp)], [to(own, ym)], []

        def across(self):
            self.across_cp.wait_recv()
            other = self.piece(1 - xh, y)
            self.up.append(to(other, yp))
            self.down.append(to(other, ym))

        def relay(self, i):
            k = xh if i == 0 else 1 - xh
            self.up[i].wait_recv()
            self.rest.append(to(self.piece(k, y_prev, 0), yp))
            self.down[i].wait_recv()
            self.rest.append(to(self.piece(k, y_next, 1), ym))

        def done(self, i):
            for cp in self.rest[2 * i : 2 * i + 2]:
                cp.wait_recv()

    class AlongFirst:
        def __init__(self, piece):
            self.piece = piece

        def start_y(self):
            own = self.piece(xh, y)
            self.up, self.down = to(own, yp), to(own, ym)

        def start_x(self):
            self.x = [to(self.piece(xh, y), x2)]

        def near(self):
            self.up.wait_recv()
            self.x.append(to(self.piece(xh, y_prev), x2))
            self.down.wait_recv()
            self.x.append(to(self.piece(xh, y_next), x2))

        def relay(self):
            self.ru = to(self.piece(xh, y_prev, 0), yp)
            self.rd = to(self.piece(xh, y_next, 1), ym)

        def far(self):
            self.ru.wait_recv()
            self.rd.wait_recv()
            self.x.append(to(self.piece(xh, y_far), x2))

        def done(self):
            for cp in self.x:
                cp.wait_recv()

    class ColGather:
        def __init__(self, buf):
            self.buf = buf

        def start(self):
            self.side = to(self.buf.at[z, xl, co], side)

        def spread(self, c):
            if c == 0:
                self.side.wait_recv()
                self.cps = []
            self.cps.append([to(self.buf.at[z, hs[c], co], zd[k]) for k in near])

        def pair(self, c):
            for cp in self.cps[c]:
                cp.wait_recv()
            return to(self.buf.at[:, hs[c], co], mate)

    def act(k, yy):
        def step(i, carry):
            h, q = lax.div(i, 2), lax.rem(i, 2)
            gate_value = g_all[k, yy, h, q].astype(F32)
            up_value = u_all[k, yy, h, q].astype(F32)
            gelu_value, gelu_slope = gelu_parts(gate_value)
            h_all[k, yy, h, q] = (gelu_value * up_value).astype(BF16)
            val[k, yy, h, q] = gelu_value
            slope_up[k, yy, h, q] = up_value * gelu_slope
            return carry

        lax.fori_loop(0, 4, step, 0)

    def partial(c):
        h, q = qs[c]

        def tile(n, carry):
            cols = pl.ds(pl.multiple_of(n * NT, 128), NT)
            lhs = cot_all[:, h, q].reshape(256, W)
            part[c, :, :, :, cols] = dot_nn(lhs, dw_v[:, cols]).astype(BF16).reshape(2, 4, 32, NT)
            return carry

        lax.fori_loop(0, U // NT, tile, 0)

    lo, hi = pl.ds(0, 16), pl.ds(16, 16)

    class Scatter:
        def __init__(self, c):
            self.c = c

        def first(self):
            c = self.c
            self.relay_up = send(part.at[c, :, y_far, lo], ry_relay.at[c, 0], yp)
            self.relay_down = send(part.at[c, :, y_far, hi], ry_relay.at[c, 1], ym)
            direct_up = send(part.at[c, :, y_next, hi], ry_full.at[c, 0, :, hi], yp)
            direct_down = send(part.at[c, :, y_prev, lo], ry_full.at[c, 1, :, lo], ym)
            self.waits = [direct_up, direct_down]

        def second(self):
            c = self.c
            self.relay_up.wait_recv()
            sy[c, 0] = (part[c, :, y_next, 0:16].astype(F32) + ry_relay[c, 0].astype(F32)).astype(BF16)
            self.waits.append(send(sy.at[c, 0], ry_full.at[c, 0, :, lo], yp))
            self.relay_down.wait_recv()
            sy[c, 1] = (part[c, :, y_prev, 16:32].astype(F32) + ry_relay[c, 1].astype(F32)).astype(BF16)
            self.waits.append(send(sy.at[c, 1], ry_full.at[c, 1, :, hi], ym))

        def third(self):
            c = self.c
            for cp in self.waits:
                cp.wait_recv()

            def total(which):
                return (
                    part[c, which, y].astype(F32)
                    + ry_full[c, 0, which].astype(F32)
                    + ry_full[c, 1, which].astype(F32)
                )

            sx[c] = total(1 - xh).astype(BF16)
            self.across = send(sx.at[c], rx.at[c], x2)
            q_own[c] = total(xh)

        def last(self):
            c = self.c
            h, q = qs[c]
            self.across.wait_recv()
            hg_all[xh, y, h, q] = (q_own[c] + rx[c].astype(F32)).astype(BF16)

    def input_grad(c):
        h, q = qs[c]

        def step(i, carry):
            k, yy = lax.div(i, 4), lax.rem(i, 4)
            hidden_grad = hg_all[k, yy, h, q].astype(F32)
            gg_all[k, yy, h, q] = (hidden_grad * slope_up[k, yy, h, q]).astype(BF16)
            ug_all[k, yy, h, q] = (hidden_grad * val[k, yy, h, q]).astype(BF16)
            return carry

        lax.fori_loop(0, 8, step, 0)
        total = dot_nt(gg_all[:, :, h, q].reshape(256, U), gw_v[...])
        total += dot_nt(ug_all[:, :, h, q].reshape(256, U), uw_v[...])
        ig_part[c] = total.reshape(8, 32, W)

    def input_grad_mate(c):
        return send(ig_part.at[c], ig_core.at[c // 2], mate)

    def input_grad_spread(c, cp):
        cp.wait_recv()
        ig_send[c // 2] = (ig_part[c] + ig_core[c // 2]).astype(BF16)
        return [send(ig_send.at[c // 2, zs[k]], ig_recv.at[c // 2, k - 1], zd[k]) for k in near]

    def input_grad_sum(c, cps):
        total = ig_part[c, z] + ig_core[c // 2, z]
        for cp in cps:
            cp.wait_recv()
        for k in range(7):
            total += ig_recv[c // 2, k].astype(F32)
        ig_red[c // 2] = total

    def weight_grad(lhs_all, rhs_all, out):
        def tile(n, carry):
            cols = pl.ds(pl.multiple_of(n * NT, 128), NT)
            rhs = rhs_all[:, :, :, :, :, cols].reshape(1024, NT)
            out[:, cols] = dot_tn(lhs_all[...].reshape(1024, W), rhs).astype(BF16)
            return carry

        lax.fori_loop(0, U // NT, tile, 0)

    l_cot = load(0, cot_h, cot_all.at[z, xl, co])
    l_g = [load(9 + i, g_h.at[pl.ds(32 * i, 32)], g_all.at[xh, y, i // 2, i % 2]) for i in range(4)]
    l_u = [load(13 + i, u_h.at[pl.ds(32 * i, 32)], u_all.at[xh, y, i // 2, i % 2]) for i in range(4)]
    l_inp = load(1, inp_h, inp_all.at[z, xl, co])
    l_dw = load(2, dw_h, dw_v)
    l_gw = load(3, gw_h, gw_v)
    l_uw = load(4, uw_h, uw_v)

    barrier = pltpu.get_barrier_semaphore()
    for d in partners:
        pl.semaphore_signal(barrier, inc=1, device_id=d, device_id_type=MESH)
    for cp in [l_cot] + l_g + l_u + [l_inp]:
        cp.wait()
    with jax.named_scope("bar"):
        pl.semaphore_wait(barrier, len(partners))
    cot, inp = ColGather(cot_all), ColGather(inp_all)
    gate, up = AcrossFirst(whole(g_all)), AlongFirst(whole(u_all))
    rs = [Scatter(c) for c in range(4)]
    hg = [AlongFirst(chunk(hg_all, c)) for c in range(3)] + [AcrossFirst(chunk(hg_all, 3))]
    with jax.named_scope("start"):
        cot.start()
        gate.start()
        up.start_y()
        inp.start()
    with jax.named_scope("act"):
        act(xh, y)
    with jax.named_scope("cot0"):
        cot.spread(0)
        cot.spread(1)
    with jax.named_scope("upx"):
        up.start_x()
    with jax.named_scope("grelay"):
        gate.relay(0)
    with jax.named_scope("pair0"):
        m0 = cot.pair(0)
        l_dw.wait()
        m0.wait_recv()
    with jax.named_scope("p0"):
        partial(0)
        rs[0].first()
    with jax.named_scope("p1"):
        partial(1)
        rs[1].first()
    with jax.named_scope("upnear"):
        up.near()
    with jax.named_scope("B0"):
        rs[0].second()
    with jax.named_scope("pair1"):
        m1 = cot.pair(1)
        inp.spread(0)
        inp.spread(1)
        m1.wait_recv()
    with jax.named_scope("p2"):
        partial(2)
        rs[2].first()
    with jax.named_scope("B1"):
        rs[1].second()
    with jax.named_scope("act2"):
        act(xh, y_prev)
        act(xh, y_next)
    with jax.named_scope("C0"):
        rs[0].third()
    with jax.named_scope("p3"):
        partial(3)
        rs[3].first()
    with jax.named_scope("B2"):
        rs[2].second()
    with jax.named_scope("C1"):
        rs[1].third()
    with jax.named_scope("D0"):
        rs[0].last()
        hg[0].start_y()
        hg[0].start_x()
    with jax.named_scope("B3"):
        rs[3].second()
    with jax.named_scope("C2"):
        rs[2].third()
    with jax.named_scope("uprelay"):
        up.relay()
    with jax.named_scope("D1"):
        rs[1].last()
        hg[1].start_y()
        hg[1].start_x()
    with jax.named_scope("E0"):
        hg[0].near()
        hg[0].relay()
    with jax.named_scope("C3"):
        rs[3].third()
    with jax.named_scope("D2"):
        rs[2].last()
        hg[2].start_y()
        hg[2].start_x()
    with jax.named_scope("gacross"):
        gate.across()
    with jax.named_scope("F0"):
        hg[0].far()
    with jax.named_scope("E1"):
        hg[1].near()
        hg[1].relay()
    with jax.named_scope("upfar"):
        up.far()
        gate.done(0)
        act(xh, y_far)
    with jax.named_scope("D3"):
        rs[3].last()
        hg[3].start()
    with jax.named_scope("F1"):
        hg[1].far()
    with jax.named_scope("E2"):
        hg[2].near()
        hg[2].relay()
    with jax.named_scope("grelay1"):
        gate.relay(1)
    with jax.named_scope("R30"):
        hg[3].relay(0)
    with jax.named_scope("F2"):
        hg[2].far()
    with jax.named_scope("X3"):
        hg[3].across()
    with jax.named_scope("acts"):
        up.done()
        gate.done(1)
        for yy in range(4):
            act(1 - xh, yy)
    with jax.named_scope("ig0"):
        l_gw.wait()
        l_uw.wait()
        hg[0].done()
        input_grad(0)
        c0 = input_grad_mate(0)
    with jax.named_scope("R31"):
        hg[3].relay(1)
    with jax.named_scope("ig1"):
        hg[1].done()
        input_grad(1)
        z1 = input_grad_spread(1, c0)
    with jax.named_scope("ig2"):
        hg[2].done()
        input_grad(2)
        c2 = input_grad_mate(2)
    with jax.named_scope("hg3done"):
        hg[3].done(0)
        hg[3].done(1)
    with jax.named_scope("ig3"):
        input_grad(3)
        z3 = input_grad_spread(3, c2)
    with jax.named_scope("ig1sum"):
        input_grad_sum(1, z1)
        fin = send(ig_red.at[0], ig_fin, side)
    with jax.named_scope("dwg"):
        weight_grad(cot_all, h_all, dwg_o)
        outs = []
    with jax.named_scope("wg"):
        m2, m3 = inp.pair(0), inp.pair(1)
        m2.wait_recv()
        m3.wait_recv()
        weight_grad(inp_all, gg_all, gwg_o)
        weight_grad(inp_all, ug_all, uwg_o)
    with jax.named_scope("ig3sum"):
        input_grad_sum(3, z3)
    with jax.named_scope("fin"):
        fin.wait_recv()
        ig_o[...] = (ig_red[1] + ig_fin[...]).astype(BF16)
    with jax.named_scope("drain"):
        for cp in sends:
            cp.wait_send()
        for cp in outs:
            cp.wait()


def write_out(a, b, c, d, a_o, b_o, c_o, d_o, sems):
    cps = [pltpu.make_async_copy(s, o, sems.at[i]) for i, (s, o) in enumerate(((a, a_o), (b, b_o), (c, c_o), (d, d_o)))]
    for cp in cps:
        cp.start()
    for cp in cps:
        cp.wait()


def body(layer_inputs, cotangent, gate_saved, up_saved, gate_weight, up_weight, down_weight):
    any_spec = pl.BlockSpec(memory_space=pl.ANY)

    def bf(*shape):
        return pltpu.VMEM(shape, BF16)

    def f32(*shape):
        return pltpu.VMEM(shape, F32)

    input_grad, gate_grad, up_grad, down_grad = pl.pallas_call(
        kernel,
        out_shape=(
            bf(32, W),
            bf(W, U),
            bf(W, U),
            bf(W, U),
        ),
        in_specs=[any_spec] * 7,
        out_specs=[pl.BlockSpec(memory_space=pltpu.VMEM)] * 4,
        scratch_shapes=[
            bf(8, 2, 2, 32, W), bf(8, 2, 2, 32, W),
            *[bf(2, 4, 2, 2, 32, U) for _ in range(6)],
            f32(2, 4, 2, 2, 32, U), f32(2, 4, 2, 2, 32, U), bf(4, 2, 4, 32, U),
            bf(W, U), bf(W, U), bf(W, U),
            bf(4, 2, 2, 16, U), bf(4, 2, 2, 32, U), bf(4, 2, 2, 16, U), bf(4, 32, U), bf(4, 32, U), f32(4, 32, U),
            f32(4, 8, 32, W), f32(2, 8, 32, W), bf(2, 8, 32, W), bf(2, 7, 32, W), f32(2, 32, W), f32(32, W),
            pltpu.SemaphoreType.DMA((17,)),
            pltpu.SemaphoreType.DMA((N_REMOTE,)),
            pltpu.SemaphoreType.DMA((N_REMOTE,)),
        ],
        compiler_params=pltpu.CompilerParams(
            collective_id=0, has_side_effects=True, vmem_limit_bytes=56 * 2**20
        ),
        cost_estimate=pl.CostEstimate(flops=8 * 10**9, bytes_accessed=9 * 10**6, transcendentals=150000),
    )(layer_inputs, cotangent, gate_saved, up_saved, gate_weight, up_weight, down_weight.T)
    return input_grad, gate_grad, up_grad, down_grad.T


def solution(mesh):
    placed = (
        P("col", "row"),
        P("col", "row"),
        P("row", "col"),
        P("row", "col"),
        P("row", "col"),
        P("row", "col"),
        P("col", "row"),
    )
    return jax.shard_map(
        body,
        mesh=mesh,
        in_specs=placed,
        out_specs=(P("col", "row"), P("row", "col"), P("row", "col"), P("col", "row")),
        check_vma=False,
    )
```

time: 556 us -> 106 us (0.19)
  waiting for transfers between devices: 505 us -> 0 us
  Pallas kernels: 0 us -> 102 us
  matrix products: 29.7 us -> 0 us
  between operations: 14.2 us -> 0.64 us
    all_gather x5 -> x0, waiting for transfers between devices: 299 us -> none  [the longest x1 70.2 us: body(): cotangent_all = lax.all_gather(cotangent, 'col', axis=0, tiled=True)]
    reduce_scatter x2 -> x0, waiting for transfers between devices: 204 us -> none  [the longest x1 113 us: body(): lax.psum_scatter(contract_last(gate_grad_all, gate_weight) + contract_las...]
    pallas_call x0 -> x1, Pallas kernels: none -> 102 us  [body(): pl.pallas_call(kernel, out_shape=(bf(32, W), bf(W, U), bf(W, U), bf(W, U)...]
    dot_general x6 -> x0, matrix products: 29.7 us -> none  [the longest x3 17.4 us: contract_last(): lax.dot_general(first_operand, second_operand, (((1,), (1,)), ((), ())),...]
  transfers between devices with their start and end apart: 7 -> 0, of which waited for: 7 -> 0; matrix products, arithmetic and copies ran while one was open for 4% -> 0% of each run, Pallas kernels for 0% -> 0%
where the time goes in v2:
time: 106 us
  Pallas kernels  102 us (96%)
  local copies, waits for them, and re-layouts  3.8 us (4%)
    pallas_call x1, Pallas kernels, body(): pl.pallas_call(kernel, out_shape=(bf(32, W), bf(W, U), bf(W, U), bf(W, U)...  102 us
    unnamed x4, local copies, waits for them, and re-layouts  3.8 us

profile of v2, /device:TPU:1, one launch (start us, length us, event | category | flops | bytes accessed | tf_op | source)
XLA Modules:
  0.0 106.2 jit_solution(13700013440334644870)
XLA Ops:
  0.6 101.7 %shard_map.102 = (bf16[32,576]{1,0:T(8,128)(2,1)S(1)}, bf16[576,1152]{1,0:T(8,128)(2,1)S(1)}, bf16[576,1152]{1,0:T(8,128)(2,1)S(1)}, bf16[576,1152]{1,0:T(8,128)(2,1)S(1)}) custom-call(bf16[32,576]{1,0:T(8,128)(2,1)} %inp_h.1, bf16[32,576]{1,0:T(8,128)(2,1)} %cot_h.1, bf16[128,1152]{1,0:T(8,128)(2,1)} %g_h.1, bf16[128,1152]{1,0:T(8,128)(2,1)} %u_h.1, ...), custom_call_target="tpu_custom_call" | custom-call | flops 8000000000 | bytes 9000000 | tf_op jit(solution)/shard_map/pallas_call | solution.py:471
  102.4 0.6 copy.15
  103.0 1.1 copy.16
  104.1 1.1 copy.17
  105.1 1.1 copy.18

commit v3 on v2

--- a/solution.py
+++ b/solution.py
@@ -15,7 +15,6 @@
 
 W = 576
 U = 1152
-NT = 384
 N_REMOTE = 140
 
 
@@ -44,7 +43,7 @@
 def kernel(
     inp_h, cot_h, g_h, u_h, gw_h, uw_h, dw_h,
     ig_o, gwg_o, uwg_o, dwg_o,
-    cot_all, inp_all, g_all, u_all, h_all, hg_all, gg_all, ug_all, val, slope_up, part,
+    cot_all, inp_all, g_all, u_all, h_all, hg_all, gg_all, ug_all, val, slope_up, part, part32,
     dw_v, gw_v, uw_v,
     ry_relay, ry_full, sy, sx, rx, q_own,
     ig_part, ig_core, ig_send, ig_recv, ig_red, ig_fin,
@@ -74,13 +73,14 @@
 
     sends = []
 
-    def send(src, dst, device):
+    def send(src, dst, device, now=True):
         i = len(sends)
         cp = pltpu.make_async_remote_copy(
             src_ref=src, dst_ref=dst, send_sem=ssem.at[i], recv_sem=rsem.at[i],
             device_id=device, device_id_type=MESH,
         )
-        cp.start()
+        if now:
+            cp.start()
         sends.append(cp)
         return cp
 
@@ -188,13 +188,9 @@
     def partial(c):
         h, q = qs[c]
 
-        def tile(n, carry):
-            cols = pl.ds(pl.multiple_of(n * NT, 128), NT)
-            lhs = cot_all[:, h, q].reshape(256, W)
-            part[c, :, :, :, cols] = dot_nn(lhs, dw_v[:, cols]).astype(BF16).reshape(2, 4, 32, NT)
-            return carry
-
-        lax.fori_loop(0, U // NT, tile, 0)
+        total = dot_nn(cot_all[:, h, q].reshape(256, W), dw_v[...]).reshape(2, 4, 32, U)
+        part32[c] = total
+        part[c] = total.astype(BF16)
 
     lo, hi = pl.ds(0, 16), pl.ds(16, 16)
 
@@ -213,10 +209,10 @@
         def second(self):
             c = self.c
             self.relay_up.wait_recv()
-            sy[c, 0] = (part[c, :, y_next, 0:16].astype(F32) + ry_relay[c, 0].astype(F32)).astype(BF16)
+            sy[c, 0] = (part32[c, :, y_next, 0:16] + ry_relay[c, 0].astype(F32)).astype(BF16)
             self.waits.append(send(sy.at[c, 0], ry_full.at[c, 0, :, lo], yp))
             self.relay_down.wait_recv()
-            sy[c, 1] = (part[c, :, y_prev, 16:32].astype(F32) + ry_relay[c, 1].astype(F32)).astype(BF16)
+            sy[c, 1] = (part32[c, :, y_prev, 16:32] + ry_relay[c, 1].astype(F32)).astype(BF16)
             self.waits.append(send(sy.at[c, 1], ry_full.at[c, 1, :, hi], ym))
 
         def third(self):
@@ -226,7 +222,7 @@
 
             def total(which):
                 return (
-                    part[c, which, y].astype(F32)
+                    part32[c, which, y]
                     + ry_full[c, 0, which].astype(F32)
                     + ry_full[c, 1, which].astype(F32)
                 )
@@ -241,28 +237,43 @@
             self.across.wait_recv()
             hg_all[xh, y, h, q] = (q_own[c] + rx[c].astype(F32)).astype(BF16)
 
-    def input_grad(c):
-        h, q = qs[c]
-
-        def step(i, carry):
-            k, yy = lax.div(i, 4), lax.rem(i, 4)
-            hidden_grad = hg_all[k, yy, h, q].astype(F32)
-            gg_all[k, yy, h, q] = (hidden_grad * slope_up[k, yy, h, q]).astype(BF16)
-            ug_all[k, yy, h, q] = (hidden_grad * val[k, yy, h, q]).astype(BF16)
-            return carry
-
-        lax.fori_loop(0, 8, step, 0)
-        total = dot_nt(gg_all[:, :, h, q].reshape(256, U), gw_v[...])
-        total += dot_nt(ug_all[:, :, h, q].reshape(256, U), uw_v[...])
-        ig_part[c] = total.reshape(8, 32, W)
-
-    def input_grad_mate(c):
-        return send(ig_part.at[c], ig_core.at[c // 2], mate)
-
-    def input_grad_spread(c, cp):
-        cp.wait_recv()
-        ig_send[c // 2] = (ig_part[c] + ig_core[c // 2]).astype(BF16)
-        return [send(ig_send.at[c // 2, zs[k]], ig_recv.at[c // 2, k - 1], zd[k]) for k in near]
+    def input_grad(cs, k):
+        for c in cs:
+            h, q = qs[c]
+
+            def step(yy, carry, h=h, q=q):
+                hidden_grad = hg_all[k, yy, h, q].astype(F32)
+                gg_all[k, yy, h, q] = (hidden_grad * slope_up[k, yy, h, q]).astype(BF16)
+                ug_all[k, yy, h, q] = (hidden_grad * val[k, yy, h, q]).astype(BF16)
+                return carry
+
+            lax.fori_loop(0, 4, step, 0)
+
+        def rows(ref):
+            return jnp.concatenate([ref[k, :, qs[c][0], qs[c][1]].reshape(128, U) for c in cs], axis=0)
+
+        total = dot_nt(rows(gg_all), gw_v[...])
+        total += dot_nt(rows(ug_all), uw_v[...])
+        for i, c in enumerate(cs):
+            ig_part[c, pl.ds(4 * k, 4)] = total[128 * i : 128 * i + 128].reshape(4, 32, W)
+
+    def input_grad_add(c, k):
+        at = pl.ds(4 * k, 4)
+        ig_send[c // 2, at] = (ig_part[c, at] + ig_core[c // 2, at]).astype(BF16)
+
+    def input_grad_copies(c):
+        return [send(ig_send.at[c // 2, zs[k]], ig_recv.at[c // 2, k - 1], zd[k], now=False) for k in near]
+
+    def spread_some(k, cps):
+        for i, j in enumerate(near):
+
+            @pl.when(lax.div(zs[j], 4) == k)
+            def _(cp=cps[i]):
+                cp.start()
+
+    def input_grad_mate(c, k):
+        at = pl.ds(4 * k, 4)
+        return send(ig_part.at[c, at], ig_core.at[c // 2, at], mate)
 
     def input_grad_sum(c, cps):
         total = ig_part[c, z] + ig_core[c // 2, z]
@@ -273,13 +284,7 @@
         ig_red[c // 2] = total
 
     def weight_grad(lhs_all, rhs_all, out):
-        def tile(n, carry):
-            cols = pl.ds(pl.multiple_of(n * NT, 128), NT)
-            rhs = rhs_all[:, :, :, :, :, cols].reshape(1024, NT)
-            out[:, cols] = dot_tn(lhs_all[...].reshape(1024, W), rhs).astype(BF16)
-            return carry
-
-        lax.fori_loop(0, U // NT, tile, 0)
+        out[...] = dot_tn(lhs_all[...].reshape(1024, W), rhs_all[...].reshape(1024, U)).astype(BF16)
 
     l_cot = load(0, cot_h, cot_all.at[z, xl, co])
     l_g = [load(9 + i, g_h.at[pl.ds(32 * i, 32)], g_all.at[xh, y, i // 2, i % 2]) for i in range(4)]
@@ -369,12 +374,12 @@
         hg[0].relay()
     with jax.named_scope("C3"):
         rs[3].third()
+    with jax.named_scope("gacross"):
+        gate.across()
     with jax.named_scope("D2"):
         rs[2].last()
         hg[2].start_y()
         hg[2].start_x()
-    with jax.named_scope("gacross"):
-        gate.across()
     with jax.named_scope("F0"):
         hg[0].far()
     with jax.named_scope("E1"):
@@ -400,33 +405,44 @@
         hg[2].far()
     with jax.named_scope("X3"):
         hg[3].across()
+    with jax.named_scope("lw"):
+        l_gw.wait()
+        l_uw.wait()
+    with jax.named_scope("igown"):
+        input_grad([0, 1, 2], xh)
+        m0a, m2a = input_grad_mate(0, xh), input_grad_mate(2, xh)
+        z1 = input_grad_copies(1)
+        m0a.wait_recv()
+        input_grad_add(1, xh)
+        spread_some(xh, z1)
+    with jax.named_scope("R31"):
+        hg[3].relay(1)
     with jax.named_scope("acts"):
         up.done()
         gate.done(1)
         for yy in range(4):
             act(1 - xh, yy)
-    with jax.named_scope("ig0"):
-        l_gw.wait()
-        l_uw.wait()
-        hg[0].done()
-        input_grad(0)
-        c0 = input_grad_mate(0)
-    with jax.named_scope("R31"):
-        hg[3].relay(1)
-    with jax.named_scope("ig1"):
-        hg[1].done()
-        input_grad(1)
-        z1 = input_grad_spread(1, c0)
-    with jax.named_scope("ig2"):
-        hg[2].done()
-        input_grad(2)
-        c2 = input_grad_mate(2)
-    with jax.named_scope("hg3done"):
+    with jax.named_scope("igother"):
+        for c in range(3):
+            hg[c].done()
+        input_grad([0, 1, 2], 1 - xh)
+        m0b, m2b = input_grad_mate(0, 1 - xh), input_grad_mate(2, 1 - xh)
+        m0b.wait_recv()
+        input_grad_add(1, 1 - xh)
+        spread_some(1 - xh, z1)
+    with jax.named_scope("ig3own"):
         hg[3].done(0)
+        input_grad([3], xh)
+        m2a.wait_recv()
+        z3 = input_grad_copies(3)
+        input_grad_add(3, xh)
+        spread_some(xh, z3)
+    with jax.named_scope("ig3b"):
         hg[3].done(1)
-    with jax.named_scope("ig3"):
-        input_grad(3)
-        z3 = input_grad_spread(3, c2)
+        input_grad([3], 1 - xh)
+        m2b.wait_recv()
+        input_grad_add(3, 1 - xh)
+        spread_some(1 - xh, z3)
     with jax.named_scope("ig1sum"):
         input_grad_sum(1, z1)
         fin = send(ig_red.at[0], ig_fin, side)
@@ -481,7 +497,7 @@
         scratch_shapes=[
             bf(8, 2, 2, 32, W), bf(8, 2, 2, 32, W),
             *[bf(2, 4, 2, 2, 32, U) for _ in range(6)],
-            f32(2, 4, 2, 2, 32, U), f32(2, 4, 2, 2, 32, U), bf(4, 2, 4, 32, U),
+            f32(2, 4, 2, 2, 32, U), f32(2, 4, 2, 2, 32, U), bf(4, 2, 4, 32, U), f32(4, 2, 4, 32, U),
             bf(W, U), bf(W, U), bf(W, U),
             bf(4, 2, 2, 16, U), bf(4, 2, 2, 32, U), bf(4, 2, 2, 16, U), bf(4, 32, U), bf(4, 32, U), f32(4, 32, U),
             f32(4, 8, 32, W), f32(2, 8, 32, W), bf(2, 8, 32, W), bf(2, 7, 32, W), f32(2, 32, W), f32(32, W),

time: 106 us -> 104 us (0.981); the launches traced: 106 us -> 103 us
  Pallas kernels: 102 us -> 98.7 us
    pallas_call x1, Pallas kernels: 102 us -> 98.7 us  [body(): pl.pallas_call(kernel, out_shape=(bf(32, W), bf(W, U), bf(W, U), bf(W, U)...]
where the time goes in v3:
time: 104 us; the launch traced here: 103 us
  Pallas kernels  98.7 us (95%)
  local copies, waits for them, and re-layouts  3.8 us (4%)
    pallas_call x1, Pallas kernels, body(): pl.pallas_call(kernel, out_shape=(bf(32, W), bf(W, U), bf(W, U), bf(W, U)...  98.7 us
    unnamed x4, local copies, waits for them, and re-layouts  3.8 us

profile of v3, /device:TPU:1, one launch (start us, length us, event | category | flops | bytes accessed | tf_op | source)
XLA Modules:
  0.0 103.1 jit_solution(898951402046025991)
XLA Ops:
  0.6 98.7 %shard_map.102 = (bf16[32,576]{1,0:T(8,128)(2,1)S(1)}, bf16[576,1152]{1,0:T(8,128)(2,1)S(1)}, bf16[576,1152]{1,0:T(8,128)(2,1)S(1)}, bf16[576,1152]{1,0:T(8,128)(2,1)S(1)}) custom-call(bf16[32,576]{1,0:T(8,128)(2,1)} %inp_h.1, bf16[32,576]{1,0:T(8,128)(2,1)} %cot_h.1, bf16[128,1152]{1,0:T(8,128)(2,1)} %g_h.1, bf16[128,1152]{1,0:T(8,128)(2,1)} %u_h.1, ...), custom_call_target="tpu_custom_call" | custom-call | flops 8000000000 | bytes 9000000 | tf_op jit(solution)/shard_map/pallas_call | solution.py:487
  99.3 0.6 copy.15
  99.9 1.1 %copy.16 = bf16[576,1152]{1,0:T(8,128)(2,1)} copy(bf16[576,1152]{1,0:T(8,128)(2,1)S(1)} %get-tuple-element.13) | data formatting | bytes 2654208
  101.0 1.1 %copy.17 = bf16[576,1152]{1,0:T(8,128)(2,1)} copy(bf16[576,1152]{1,0:T(8,128)(2,1)S(1)} %get-tuple-element.14) | data formatting | bytes 2654208
  102.0 1.1 %copy.18 = bf16[1152,576]{0,1:T(8,128)(2,1)} copy(bf16[1152,576]{0,1:T(8,128)(2,1)S(1)} %bitcast.2) | data formatting | bytes 2654208

commit v4 on v3

--- a/solution.py
+++ b/solution.py
@@ -382,13 +382,13 @@
         hg[2].start_x()
     with jax.named_scope("F0"):
         hg[0].far()
-    with jax.named_scope("E1"):
-        hg[1].near()
-        hg[1].relay()
     with jax.named_scope("upfar"):
         up.far()
         gate.done(0)
         act(xh, y_far)
+    with jax.named_scope("E1"):
+        hg[1].near()
+        hg[1].relay()
     with jax.named_scope("D3"):
         rs[3].last()
         hg[3].start()
@@ -443,17 +443,18 @@
         m2b.wait_recv()
         input_grad_add(3, 1 - xh)
         spread_some(1 - xh, z3)
-    with jax.named_scope("ig1sum"):
-        input_grad_sum(1, z1)
-        fin = send(ig_red.at[0], ig_fin, side)
     with jax.named_scope("dwg"):
         weight_grad(cot_all, h_all, dwg_o)
         outs = []
-    with jax.named_scope("wg"):
+    with jax.named_scope("gate_wg"):
         m2, m3 = inp.pair(0), inp.pair(1)
         m2.wait_recv()
         m3.wait_recv()
         weight_grad(inp_all, gg_all, gwg_o)
+    with jax.named_scope("ig1sum"):
+        input_grad_sum(1, z1)
+        fin = send(ig_red.at[0], ig_fin, side)
+    with jax.named_scope("up_wg"):
         weight_grad(inp_all, ug_all, uwg_o)
     with jax.named_scope("ig3sum"):
         input_grad_sum(3, z3)

time: 104 us -> 103 us (level)
  no operation moved by 1% of the time
where the time goes in v4:
time: 103 us
  Pallas kernels  98.7 us (96%)
  local copies, waits for them, and re-layouts  3.8 us (4%)
    pallas_call x1, Pallas kernels, body(): pl.pallas_call(kernel, out_shape=(bf(32, W), bf(W, U), bf(W, U), bf(W, U)...  98.7 us
    unnamed x4, local copies, waits for them, and re-layouts  3.8 us

profile of v4, /device:TPU:1, one launch (start us, length us, event | category | flops | bytes accessed | tf_op | source)
XLA Modules:
  0.0 103.1 jit_solution(13687669938124512375)
XLA Ops:
  0.6 98.7 %shard_map.102 = (bf16[32,576]{1,0:T(8,128)(2,1)S(1)}, bf16[576,1152]{1,0:T(8,128)(2,1)S(1)}, bf16[576,1152]{1,0:T(8,128)(2,1)S(1)}, bf16[576,1152]{1,0:T(8,128)(2,1)S(1)}) custom-call(bf16[32,576]{1,0:T(8,128)(2,1)} %inp_h.1, bf16[32,576]{1,0:T(8,128)(2,1)} %cot_h.1, bf16[128,1152]{1,0:T(8,128)(2,1)} %g_h.1, bf16[128,1152]{1,0:T(8,128)(2,1)} %u_h.1, ...), custom_call_target="tpu_custom_call" | custom-call | flops 8000000000 | bytes 9000000 | tf_op jit(solution)/shard_map/pallas_call | solution.py:488
  99.3 0.6 copy.15
  99.9 1.1 %copy.16 = bf16[576,1152]{1,0:T(8,128)(2,1)} copy(bf16[576,1152]{1,0:T(8,128)(2,1)S(1)} %get-tuple-element.13) | data formatting | bytes 2654208
  101.0 1.1 %copy.17 = bf16[576,1152]{1,0:T(8,128)(2,1)} copy(bf16[576,1152]{1,0:T(8,128)(2,1)S(1)} %get-tuple-element.14) | data formatting | bytes 2654208
  102.0 1.1 %copy.18 = bf16[1152,576]{0,1:T(8,128)(2,1)} copy(bf16[1152,576]{0,1:T(8,128)(2,1)S(1)} %bitcast.2) | data formatting | bytes 2654208
